TPU v7x, 128 devices: a whole 4x4x4 slice. The times are simulated.
128 devices in a mesh: tm: 8 (over x, core), mem: 16 (over y, z).
Axes of the slice: x: 4, y: 4, z: 4, core: 2. Of those that a mesh axis runs over, the one named last changes fastest.
Arguments:
- tokens: bfloat16 [32768, 2048], P(('tm', 'mem')), may hold values from -6 to 6
- queries: bfloat16 [32768, 2048], P(('tm', 'mem')), may hold values from -6 to 6
- log_decay: bfloat16 [32768, 16], P(('tm', 'mem')), may hold values from -1 to 0
- route_ids: int32 [32768, 2], P(('tm', 'mem')), may hold values from 0 to 15, all different within a row; in each aligned block of 256 rows (0 to 255, 256 to 511, ...) at most 48 rows name the same one
- gate_weights: float32 [32768, 2], P(('tm', 'mem')), may hold values from 0.3 to 1
- kv_weight: bfloat16 [16, 2048, 4096], P('mem'), may hold values from -0.125 to 0.125
Outputs:
- mixed: bfloat16 [32768, 2048], P(('tm', 'mem'))
Inputs may be any that keep to these rules, and one draw needn't show every extreme that they name: `route_ids`: each row names 2 different memories. In each aligned block of 256 rows (the rows of one device) no memory is named by more than 48 rows, and in some block one memory is named by exactly 48 rows.
All inputs are finite; a program needn't handle non-finite values.
Results may differ from a plain program's by a relative error of at most 0.006.
Values may be sent and summed in bfloat16 or wider, within the bound.
A program may use at most 128 MiB of HBM per device.

v0:
```python
import math

import jax
import jax.numpy as jnp
from jax import lax
from jax.sharding import PartitionSpec as P

exact_mode = lax.Precision.HIGHEST


def prefix(part, axis, combine, identity):
    place = lax.axis_index(axis)
    gathered = jax.tree.map(lambda a: lax.all_gather(a, axis), part)
    state = jax.tree.map(lambda a, e: jnp.zeros_like(a) + jnp.asarray(e, a.dtype), part, identity)

    def one(turn, state):
        return combine(
            state, jax.tree.map(lambda a: lax.dynamic_index_in_dim(a, turn, 0, False), gathered)
        )

    return lax.fori_loop(0, place, one, state)


def block_pass(queries_heads, keys_heads, values_heads, decay_logs, block_rows):
    head_count, chain_rows, head_size = queries_heads.shape
    block_count = chain_rows // block_rows

    def split_blocks(tensor):
        return jnp.moveaxis(tensor.reshape(head_count, block_count, block_rows, head_size), 1, 0)

    blocked = (
        split_blocks(queries_heads),
        split_blocks(keys_heads),
        split_blocks(values_heads),
        jnp.moveaxis(decay_logs.reshape(head_count, block_count, block_rows), 1, 0),
    )
    lower = jnp.arange(block_rows)[:, None] >= jnp.arange(block_rows)[None, :]

    def advance(carried, pieces):
        query_block, key_block, value_block, log_block = pieces
        running = jnp.cumsum(log_block, axis=1)
        spread = jnp.minimum(running[:, :, None] - running[:, None, :], 0.0)
        weights = jnp.where(lower[None], jnp.exp(spread), 0.0)
        scores = (
            jnp.einsum("hnd,hid->hni", query_block, key_block, preferred_element_type=jnp.float32)
            * weights
        )
        value_wide = value_block.astype(jnp.float32)
        within = jnp.einsum("hni,hie->hne", scores, value_wide, precision=exact_mode)
        earlier = (
            jnp.einsum(
                "hnd,hde->hne", query_block.astype(jnp.float32), carried, precision=exact_mode
            )
            * jnp.exp(running)[:, :, None]
        )
        ending = running[:, -1]
        fading = jnp.exp(ending[:, None] - running)
        carried = jnp.exp(ending)[:, None, None] * carried + jnp.einsum(
            "hid,hie->hde",
            key_block.astype(jnp.float32) * fading[:, :, None],
            value_wide,
            precision=exact_mode,
        )
        return (carried, within + earlier)

    start = jnp.zeros((head_count, head_size, head_size), jnp.float32)
    final_state, outputs = lax.scan(advance, start, blocked)
    outputs = jnp.moveaxis(outputs, 0, 1).reshape(head_count, chain_rows, head_size)
    return (final_state, outputs)


def normalize(outputs):
    mean_square = jnp.mean(outputs * outputs, axis=-1, keepdims=True)
    return outputs * lax.rsqrt(mean_square + 1e-06)


def link(earlier_pair, later_pair):
    return (
        earlier_pair[0] + later_pair[0],
        jnp.exp(later_pair[0])[:, None, None] * earlier_pair[1] + later_pair[1],
    )


def on_device(tokens, queries, log_decay, route_ids, gate_weights, kv_weight):
    tok_rows, model_width = tokens.shape
    head_count = log_decay.shape[1]
    head_size = model_width // head_count
    top_count = route_ids.shape[1]
    members = lax.axis_size("mem")
    capacity = 3 * tok_rows * top_count // (2 * members)
    chain_rows = members * capacity
    flat_ids = route_ids.reshape(-1)
    onehot = (flat_ids[:, None] == jnp.arange(members, dtype=jnp.int32)[None, :]).astype(jnp.int32)
    before = jnp.cumsum(onehot, axis=0) - onehot
    position = jnp.sum(before * onehot, axis=1)
    slot_index = flat_ids * capacity + position
    source_row = jnp.arange(flat_ids.shape[0], dtype=jnp.int32) // top_count
    slot_token = jnp.full((chain_rows,), tok_rows, jnp.int32).at[slot_index].set(source_row)
    padded_tokens = jnp.concatenate([tokens, jnp.zeros((1, model_width), jnp.bfloat16)], axis=0)
    padded_queries = jnp.concatenate([queries, jnp.zeros((1, model_width), jnp.bfloat16)], axis=0)
    padded_decay = jnp.concatenate([log_decay, jnp.zeros((1, head_count), jnp.bfloat16)], axis=0)
    send_tokens = padded_tokens[slot_token].reshape(members, capacity, model_width)
    send_queries = padded_queries[slot_token].reshape(members, capacity, model_width)
    send_decay = padded_decay[slot_token].reshape(members, capacity, head_count)
    received_tokens, received_queries, received_decay = (
        lax.all_to_all(send_tokens, "mem", split_axis=0, concat_axis=0, tiled=True),
        lax.all_to_all(send_queries, "mem", split_axis=0, concat_axis=0, tiled=True),
        lax.all_to_all(send_decay, "mem", split_axis=0, concat_axis=0, tiled=True),
    )
    chain_x = received_tokens.reshape(chain_rows, model_width)
    projected = jnp.dot(chain_x, kv_weight[0], preferred_element_type=jnp.float32).astype(
        jnp.bfloat16
    )
    keys_heads = (
        projected[:, :model_width].reshape(chain_rows, head_count, head_size).transpose(1, 0, 2)
    )
    values_heads = (
        projected[:, model_width:].reshape(chain_rows, head_count, head_size).transpose(1, 0, 2)
    )
    keys_heads, values_heads = (keys_heads, values_heads)
    query_heads = received_queries.reshape(chain_rows, head_count, head_size).transpose(1, 0, 2)
    logs_heads = received_decay.reshape(chain_rows, head_count).astype(jnp.float32).T
    block_rows = math.gcd(chain_rows, 512)
    final_local, local_out = block_pass(
        query_heads, keys_heads, values_heads, logs_heads, block_rows
    )
    total_log = jnp.sum(logs_heads, axis=1)
    identity = (
        jnp.zeros((head_count,), jnp.float32),
        jnp.zeros((head_count, head_size, head_size), jnp.float32),
    )
    incoming_log, incoming = prefix((total_log, final_local), "tm", link, identity)
    through = jnp.cumsum(logs_heads, axis=1)
    outputs = local_out + jnp.exp(through)[:, :, None] * jnp.einsum(
        "hnd,hde->hne", query_heads.astype(jnp.float32), incoming, precision=exact_mode
    )
    normed = (
        normalize(outputs)
        .astype(jnp.bfloat16)
        .transpose(1, 0, 2)
        .reshape(members, capacity, model_width)
    )
    returned = lax.all_to_all(normed, "mem", split_axis=0, concat_axis=0, tiled=True)
    picked = returned.reshape(chain_rows, model_width)[slot_index].astype(jnp.float32)
    picked = picked.reshape(tok_rows, top_count, model_width)
    mixed = jnp.sum(gate_weights[:, :, None] * picked, axis=1)
    return mixed.astype(jnp.bfloat16)


def solution(mesh):
    placed = (
        P(("tm", "mem"), None),
        P(("tm", "mem"), None),
        P(("tm", "mem"), None),
        P(("tm", "mem"), None),
        P(("tm", "mem"), None),
        P("mem", None, None),
    )
    return jax.shard_map(
        on_device, mesh=mesh, in_specs=placed, out_specs=P(("tm", "mem"), None), check_vma=False
    )
```

profile of v0, /device:TPU:87, one launch (start us, length us, event | category | flops | bytes accessed | tf_op | source)
XLA Modules:
  0.0 331.0 jit_solution(8816478148201656392)
XLA Ops:
  16.3 6.8 %all-to-all-start = ((bf16[16,2,384]{2,1,0:T(2,128)(2,1)}), bf16[16,2,384]{2,1,0:T(2,128)(2,1)S(1)}, u32[]{:S(2)}, u32[]{:S(2)}) async-start(bf16[16,2,384]{2,1,0:T(2,128)(2,1)} %reshape.280), calls=%async_computation | async-start | bytes 49152 | tf_op jit(solution)/shard_map/all_to_all | solution.py:108
  23.3 4.3 %gather_fusion.1 = bf16[768,2048]{1,0:T(8,128)(2,1)} fusion(bf16[257,2048]{1,0:T(8,128)(2,1)S(1)} %concatenate.10, s32[1024]{0:T(1024)S(1)} %pad_clamp_fusion.1), kind=kCustom, calls=%fused_computation.1 | custom fusion | bytes 6294528 | tf_op jit(solution)/shard_map/gather | solution.py:102
  27.6 6.8 %all-to-all-start.1 = ((bf16[16,48,2048]{2,1,0:T(8,128)(2,1)}), bf16[16,48,2048]{2,1,0:T(8,128)(2,1)}, u32[]{:S(2)}, u32[]{:S(2)}) async-start(bf16[16,48,2048]{2,1,0:T(8,128)(2,1)} %bitcast.160), calls=%async_computation.1 | async-start | bytes 6291456 | tf_op jit(solution)/shard_map/all_to_all | solution.py:106
  34.5 4.4 %gather_fusion.2 = bf16[768,2048]{1,0:T(8,128)(2,1)} fusion(bf16[257,2048]{1,0:T(8,128)(2,1)S(1)} %concatenate.11, s32[1024]{0:T(1024)S(1)} %pad_clamp_fusion.1), kind=kCustom, calls=%fused_computation.2 | custom fusion | bytes 6294528 | tf_op jit(solution)/shard_map/gather | solution.py:103
  39.2 31.6 %all-to-all-done.1 = bf16[16,48,2048]{2,1,0:T(8,128)(2,1)} async-done(((bf16[16,48,2048]{2,1,0:T(8,128)(2,1)}), bf16[16,48,2048]{2,1,0:T(8,128)(2,1)}, u32[]{:S(2)}, u32[]{:S(2)}) %all-to-all-start.1) | async-done | bytes 3145760 | tf_op jit(solution)/shard_map/all_to_all | solution.py:106
  70.7 6.9 %all-to-all-start.2 = ((bf16[16,48,2048]{2,1,0:T(8,128)(2,1)}), bf16[16,48,2048]{2,1,0:T(8,128)(2,1)S(1)}, u32[]{:S(2)}, u32[]{:S(2)}) async-start(bf16[16,48,2048]{2,1,0:T(8,128)(2,1)} %bitcast.159), calls=%async_computation.2 | async-start | bytes 6291456 | tf_op jit(solution)/shard_map/all_to_all | solution.py:107
  78.2 17.6 %fusion.34 = bf16[768,4096]{1,0:T(8,128)(2,1)S(1)} fusion(bf16[768,2048]{1,0:T(8,128)(2,1)} %bitcast.9, bf16[1,2048,4096]{2,1,0:T(8,128)(2,1)} %param.15), kind=kOutput, calls=%fused_computation.50 | convolution fusion | flops 12888047616 | bytes 26214400 | tf_op jit(solution)/shard_map/dot_general | solution.py:111
  103.9 9.2 %all-to-all-done.2 = bf16[16,48,2048]{2,1,0:T(8,128)(2,1)S(1)} async-done(((bf16[16,48,2048]{2,1,0:T(8,128)(2,1)}), bf16[16,48,2048]{2,1,0:T(8,128)(2,1)S(1)}, u32[]{:S(2)}, u32[]{:S(2)}) %all-to-all-start.2) | async-done | bytes 3145760 | tf_op jit(solution)/shard_map/all_to_all | solution.py:107
  116.8 52.3 %while.26 = (s32[]{:T(128)}, f32[16,128,128]{2,1,0:T(8,128)}, f32[3,16,256,128]{3,2,0,1:T(8,128)}, f32[3,16,256]{2,0,1:T(4,128)S(1)}, bf16[3,16,256,128]{3,1,2,0...) while((s32[]{:T(128)}, f32[16,128,128]{2,1,0:T(8,128)}, ...), condition=%wide.region_7.8_spmd.clone, body=%wide.region_4.7_spmd.clone.sunk | while | flops 3497598976 | bytes 37063800 | solution.py:67
  129.4 4.1 %fusion.70 = f32[16,128,128]{2,1,0:T(8,128)} fusion(f32[16,256]{1,0:T(8,128)S(1)} %get-tuple-element.260, f32[16,128,128]{2,1,0:T(8,128)} %get-tuple-element.275, bf16[1,16,256,128]{3,1,2,0:T(8,128)(2,1)S(1)} %get-tuple-element.261, bf16[1,16,256,128]{3,1,2,0:T(8,128)(2,1)S(1)} %copy-done.2, f32[16]{0:T(128)S(1)} %exp.67, pred[]{:T(512)S(6)} %compare.8), kind=kOutput, calls=%fused_computation.22.clone.1 | convolution fusion | flops 807141376 | bytes 4210753 | tf_op jit(solution)/shard_map/while/body/eval_jaxpr/hid,hie->hde/dot_general | solution.py:58
  142.0 4.2 %bitcast_dynamic-update-slice_fusion.2 = f32[3,16,256,128]{3,2,0,1:T(8,128)} fusion(f32[3,16,256,128]{3,2,0,1:T(8,128)} %get-tuple-element.276, s32[]{:T(128)} %get-tuple-element.274, f32[16,256,128]{2,1,0:T(8,128)S(1)} %fusion.72, f32[16,256]{1,0:T(8,128)S(1)} %get-tuple-element.263, f32[16,128,128]{2,1,0:T(8,128)} %get-tuple-element.275, ...), kind=kOutput, calls=%fused_computation.14.clone.1 | convolution fusion | flops 806617088 | bytes 6308865 | tf_op jit(solution)/shard_map/while/body/eval_jaxpr/hnd,hde->hne/dot_general | solution.py:51
  146.2 5.1 %fusion.70 = f32[16,128,128]{2,1,0:T(8,128)} fusion(f32[16,256]{1,0:T(8,128)S(1)} %get-tuple-element.260, f32[16,128,128]{2,1,0:T(8,128)} %get-tuple-element.275, bf16[1,16,256,128]{3,1,2,0:T(8,128)(2,1)S(1)} %get-tuple-element.261, bf16[1,16,256,128]{3,1,2,0:T(8,128)(2,1)S(1)} %copy-done.2, f32[16]{0:T(128)S(1)} %exp.67, pred[]{:T(512)S(6)} %compare.8), kind=kOutput, calls=%fused_computation.22.clone.1 | convolution fusion | flops 807141376 | bytes 4210753 | tf_op jit(solution)/shard_map/while/body/eval_jaxpr/hid,hie->hde/dot_general | solution.py:58
  159.8 4.2 %bitcast_dynamic-update-slice_fusion.2 = f32[3,16,256,128]{3,2,0,1:T(8,128)} fusion(f32[3,16,256,128]{3,2,0,1:T(8,128)} %get-tuple-element.276, s32[]{:T(128)} %get-tuple-element.274, f32[16,256,128]{2,1,0:T(8,128)S(1)} %fusion.72, f32[16,256]{1,0:T(8,128)S(1)} %get-tuple-element.263, f32[16,128,128]{2,1,0:T(8,128)} %get-tuple-element.275, ...), kind=kOutput, calls=%fused_computation.14.clone.1 | convolution fusion | flops 806617088 | bytes 6308865 | tf_op jit(solution)/shard_map/while/body/eval_jaxpr/hnd,hde->hne/dot_general | solution.py:51
  164.0 5.1 %fusion.70 = f32[16,128,128]{2,1,0:T(8,128)} fusion(f32[16,256]{1,0:T(8,128)S(1)} %get-tuple-element.260, f32[16,128,128]{2,1,0:T(8,128)} %get-tuple-element.275, bf16[1,16,256,128]{3,1,2,0:T(8,128)(2,1)S(1)} %get-tuple-element.261, bf16[1,16,256,128]{3,1,2,0:T(8,128)(2,1)S(1)} %copy-done.2, f32[16]{0:T(128)S(1)} %exp.67, pred[]{:T(512)S(6)} %compare.8), kind=kOutput, calls=%fused_computation.22.clone.1 | convolution fusion | flops 807141376 | bytes 4210753 | tf_op jit(solution)/shard_map/while/body/eval_jaxpr/hid,hie->hde/dot_general | solution.py:58
  170.6 14.4 %all-reduce.3 = f32[128]{0:T(128)S(1)} all-reduce(f32[128]{0:T(128)S(1)} %dynamic-update-slice), channel_id=2, replica_groups=mesh['tm'=8,'mem'=16] {'tm'}, use_global_device_ids=true, to_apply=%add.3 | all-reduce | flops 128 | bytes 1024
  187.1 6.8 %copy.107 = f32[16,768,128]{1,2,0:T(8,128)} copy(f32[16,768,128]{2,1,0:T(8,128)} %bitcast.161) | data formatting | bytes 12582912 | tf_op jit(solution)/shard_map/reshape | solution.py:68
  194.0 29.8 %all-gather.4.cloned.1.call-done = f32[128,128,128]{2,1,0:T(8,128)} async-done(((f32[16,128,128]{2,1,0:T(8,128)}), f32[128,128,128]{2,1,0:T(8,128)}) %all-gather.4.cloned.1.call-update) | async-done | bytes 8388624 | tf_op jit(solution)/shard_map/all_gather | solution.py:13
  223.9 10.7 %while.25 = (s32[]{:T(128)}, f32[16,128,128]{2,1,0:T(8,128)S(1)}, s32[]{:T(128)}, f32[8,16]{1,0:T(8,128)S(1)}, f32[8,16,128,128]{3,2,1,0:T(8,128)}, /*index=5*/s32[]{:T(128)}, s32[]{:T(128)}, s32[]{:T(128)}) while((s32[]{:T(128)}, f32[16,128,128]{2,1,0:T(8,128)S(1)}, s32[]{:T(128)}, f32[8,16]{1,0:T(8,128)S(1)}, ...), condition=%wide.region_12.13_spmd, body=%wide.region_11.12_spmd.sunk | while | flops 524293 | bytes 3146047 | solution.py:21
  234.6 8.0 %multiply_reduce_fusion = (f32[16,768]{1,0:T(8,128)S(1)}, f32[16,768,128]{1,2,0:T(8,128)S(1)}) fusion(f32[16,768,128]{1,2,0:T(8,128)} %copy.107, f32[16,128,128]{2,1,0:T(8,128)S(1)} %get-tuple-element.94, bf16[768,16,128]{2,1,0:T(8,128)(2,1)} %bitcast.155, f32[16,768]{1,0:T(8,128)S(1)} %copy_bitcast_fusion.8), kind=kOutput, calls=%fused_computation.52 | convolution fusion | flops 2422198272 | bytes 16875520 | tf_op jit(solution)/shard_map/hnd,hde->hne/dot_general | solution.py:134
  245.0 4.1 %copy.108 = bf16[768,16,128]{2,1,0:T(8,128)(2,1)S(1)} copy(bf16[768,16,128]{0,2,1:T(8,128)(2,1)} %fusion.37) | data formatting | bytes 6291456 | tf_op jit(solution)/shard_map/transpose | solution.py:140
  252.5 7.1 %all-to-all-start.3 = ((bf16[16,48,2048]{2,1,0:T(8,128)(2,1)}), bf16[16,48,2048]{2,1,0:T(8,128)(2,1)S(1)}, u32[]{:S(2)}, u32[]{:S(2)}) async-start(bf16[16,48,2048]{2,1,0:T(8,128)(2,1)} %reshape.218), calls=%async_computation.3 | async-start | bytes 6291456 | tf_op jit(solution)/shard_map/all_to_all | solution.py:143
  259.8 45.5 %all-to-all-done.3 = bf16[16,48,2048]{2,1,0:T(8,128)(2,1)S(1)} async-done(((bf16[16,48,2048]{2,1,0:T(8,128)(2,1)}), bf16[16,48,2048]{2,1,0:T(8,128)(2,1)S(1)}, u32[]{:S(2)}, u32[]{:S(2)}) %all-to-all-start.3) | async-done | bytes 3145760 | tf_op jit(solution)/shard_map/all_to_all | solution.py:143
  308.6 5.4 %reshape.220 = f32[256,2,2048]{2,1,0:T(2,128)} reshape(bf16[512,2048]{1,0:T(8,128)(2,1)} %gather_fusion.3) | data formatting | bytes 6291456 | tf_op jit(solution)/shard_map/convert_element_type | solution.py:144
  314.0 9.9 %multiply_reduce_fusion.1 = bf16[256,2048]{1,0:T(8,128)(2,1)} fusion(f32[256,2,2048]{2,1,0:T(2,128)} %reshape.220, f32[256,2]{1,0:T(8,128)S(1)} %copy.88), kind=kLoop, calls=%fused_computation.54 | loop fusion | flops 1572864 | bytes 5244928 | tf_op jit(solution)/shard_map/reduce_sum | solution.py:146
  (134 shorter events, 74.3 us)
Async XLA Ops:
  6.5 16.6 %copy-start.3 = (bf16[256,2048]{1,0:T(8,128)(2,1)S(1)}, bf16[256,2048]{1,0:T(8,128)(2,1)}, u32[]{:S(2)}) copy-start(bf16[256,2048]{1,0:T(8,128)(2,1)} %param.10) | copy-start | bytes 3145732
  16.3 11.2 %all-to-all-start = ((bf16[16,2,384]{2,1,0:T(2,128)(2,1)}), bf16[16,2,384]{2,1,0:T(2,128)(2,1)S(1)}, u32[]{:S(2)}, u32[]{:S(2)}) async-start(bf16[16,2,384]{2,1,0:T(2,128)(2,1)} %reshape.280), calls=%async_computation | async-start | bytes 49152 | tf_op jit(solution)/shard_map/all_to_all | solution.py:108
  27.6 6.8 %copy-start.4 = (bf16[256,2048]{1,0:T(8,128)(2,1)S(1)}, bf16[256,2048]{1,0:T(8,128)(2,1)}, u32[]{:S(2)}) copy-start(bf16[256,2048]{1,0:T(8,128)(2,1)} %param.11) | copy-start | bytes 3145732
  27.6 43.2 %all-to-all-start.1 = ((bf16[16,48,2048]{2,1,0:T(8,128)(2,1)}), bf16[16,48,2048]{2,1,0:T(8,128)(2,1)}, u32[]{:S(2)}, u32[]{:S(2)}) async-start(bf16[16,48,2048]{2,1,0:T(8,128)(2,1)} %bitcast.160), calls=%async_computation.1 | async-start | bytes 6291456 | tf_op jit(solution)/shard_map/all_to_all | solution.py:106
  70.7 42.4 %all-to-all-start.2 = ((bf16[16,48,2048]{2,1,0:T(8,128)(2,1)}), bf16[16,48,2048]{2,1,0:T(8,128)(2,1)S(1)}, u32[]{:S(2)}, u32[]{:S(2)}) async-start(bf16[16,48,2048]{2,1,0:T(8,128)(2,1)} %bitcast.159), calls=%async_computation.2 | async-start | bytes 6291456 | tf_op jit(solution)/shard_map/all_to_all | solution.py:107
  77.7 146.1 %all-gather.4.cloned.1.call-start = ((), (), s32[]{:S(2)}) async-start(), calls=%async_computation.4 | async-start | bytes 9437184 | tf_op jit(solution)/shard_map/all_gather | solution.py:13
  114.1 2.7 copy-start
  116.8 52.3 %copy-start.6 = (u32[128]{0:T(128)S(1)}, u32[128]{0:T(128)}, u32[]{:S(2)}) copy-start(u32[128]{0:T(128)} %constant.96) | copy-start | bytes 1540
  119.8 2.4 copy-start.1
  125.5 3.9 %copy-start.2 = (bf16[1,16,256,128]{3,1,2,0:T(8,128)(2,1)S(1)}, bf16[1,16,256,128]{3,1,2,0:T(8,128)(2,1)}, u32[]{:S(2)}) copy-start(bf16[1,16,256,128]{3,1,2,0:T(8,128)(2,1)} %copy-done.1) | copy-start | bytes 3145732 | tf_op jit(solution)/shard_map/while
  136.3 2.4 copy-start.1
  142.0 4.2 %copy-start.2 = (bf16[1,16,256,128]{3,1,2,0:T(8,128)(2,1)S(1)}, bf16[1,16,256,128]{3,1,2,0:T(8,128)(2,1)}, u32[]{:S(2)}) copy-start(bf16[1,16,256,128]{3,1,2,0:T(8,128)(2,1)} %copy-done.1) | copy-start | bytes 3145732 | tf_op jit(solution)/shard_map/while
  154.1 2.4 copy-start.1
  159.8 4.2 %copy-start.2 = (bf16[1,16,256,128]{3,1,2,0:T(8,128)(2,1)S(1)}, bf16[1,16,256,128]{3,1,2,0:T(8,128)(2,1)}, u32[]{:S(2)}) copy-start(bf16[1,16,256,128]{3,1,2,0:T(8,128)(2,1)} %copy-done.1) | copy-start | bytes 3145732 | tf_op jit(solution)/shard_map/while
  252.5 7.1 %copy-start.5 = (f32[256,2]{0,1:T(2,128)S(1)}, f32[256,2]{0,1:T(2,128)}, u32[]{:S(2)}) copy-start(f32[256,2]{0,1:T(2,128)} %param.14) | copy-start | bytes 6148
  252.5 52.8 %all-to-all-start.3 = ((bf16[16,48,2048]{2,1,0:T(8,128)(2,1)}), bf16[16,48,2048]{2,1,0:T(8,128)(2,1)S(1)}, u32[]{:S(2)}, u32[]{:S(2)}) async-start(bf16[16,48,2048]{2,1,0:T(8,128)(2,1)} %reshape.218), calls=%async_computation.3 | async-start | bytes 6291456 | tf_op jit(solution)/shard_map/all_to_all | solution.py:143
Sparse Core Ops, SparseCore 0:
  169.2 54.5 all-gather.3
where the time goes:
time: 337 us; the launch traced here: 331 us
  waiting for transfers between devices  116 us (34%)
  matrix products  68.2 us (20%)
  local copies, waits for them, and re-layouts  59.8 us (18%)
  other arithmetic  28.8 us (9%)
  starting transfers between devices  28.3 us (8%)
  between operations  14.5 us (4%)
  blocking collectives  14.4 us (4%)
    all_to_all x1, waiting for transfers between devices, on_device(): lax.all_to_all(normed, 'mem', split_axis=0, concat_axis=0, tiled=True)  45.5 us
    all_to_all x1, waiting for transfers between devices, on_device(): lax.all_to_all(send_tokens, 'mem', split_axis=0, concat_axis=0, tiled=True)  31.6 us
    all_gather x1, waiting for transfers between devices, prefix(): gathered = jax.tree.map(lambda a: lax.all_gather(a, axis), part)  29.8 us
    dot_general x1, matrix products, on_device(): jnp.dot(chain_x, kv_weight[0], preferred_element_type=jnp.float32)  17.6 us
    unnamed x1, blocking collectives  14.4 us
    dot_general x3, matrix products, advance(): jnp.einsum('hid,hie->hde', key_block.astype(jnp.float32) * fading[:, :, N...  14.3 us
    unnamed x22, local copies, waits for them, and re-layouts  12.5 us
    dot_general x3, matrix products, advance(): jnp.einsum('hnd,hde->hne', query_block.astype(jnp.float32), carried, prec...  12.2 us
  transfers between devices with their start and end apart: 5, of which 4 were waited for; matrix products, arithmetic and copies ran while one was open for 14% of the time, Pallas kernels for 0%

commit v1 on v0

v1 whole, which is shorter than its diff:
```python
import functools

import jax
import jax.numpy as jnp
from jax import lax
from jax.experimental import pallas as pl
from jax.experimental.pallas import tpu as pltpu
from jax.sharding import PartitionSpec as P

MESH = pl.DeviceIdType.MESH
F32, BF16 = jnp.float32, jnp.bfloat16

MEM_Y, MEM_Z = 4, 4
MEMBERS = MEM_Y * MEM_Z
TM = 8
TOK = 256
CAP = 48
ROWS = MEMBERS * CAP
D = 2048
H = 16
HD = 128
XW = D + 128
CHUNK = 256
CHUNKS = ROWS // CHUNK
GROUPS = 4
GW = D // GROUPS
GH = H // GROUPS
PAIRS = H // 2
GP = PAIRS // GROUPS

SHIFTS = (
    (1, 0), (3, 0), (0, 1), (0, 3),
    (1, 1), (3, 3), (1, 3), (3, 1),
    (2, 1), (2, 3), (1, 2), (3, 2),
    (2, 0), (0, 2), (2, 2),
)
PEERS = len(SHIFTS)
BACK = 3


def mm(a, b, da=1, db=0):
    return lax.dot_general(a, b, (((da,), (db,)), ((), ())), preferred_element_type=F32)


def kernel(
    tok_hbm, qry_hbm, dec_ref, route_ref, gate_ref, w_hbm, out_hbm,
    tok, qry, w, onehot, chi, clo,
    sendx, recvx, sendq, recvq, kb, vb, osend, ret, outb,
    rcol, rrow, ends, atot, aprev, ub, inc, exc, ssend, srecv,
    load_sem, xs, xr, qs, qr, os_, or_, as_, ar, ss, sr, out_sem,
):
    tm = lax.axis_index("tm")
    me = lax.axis_index("mem")
    my, mz = lax.div(me, MEM_Z), lax.rem(me, MEM_Z)

    def at(dy, dz):
        return lax.rem(my + dy, MEM_Y) * MEM_Z + lax.rem(mz + dz, MEM_Z)

    to = [at(dy, dz) for dy, dz in SHIFTS]
    source = [at(MEM_Y - dy, MEM_Z - dz) for dy, dz in SHIFTS]

    def block(place):
        return pl.ds(pl.multiple_of(place * CAP, 16), CAP)

    barrier = pltpu.get_barrier_semaphore()
    for i in range(PEERS):
        pl.semaphore_signal(barrier, inc=1, device_id=(tm, to[i]), device_id_type=MESH)
    for d in range(1, TM):
        pl.semaphore_signal(
            barrier, inc=1, device_id=(lax.rem(tm + d, TM), me), device_id_type=MESH
        )

    load_tok = pltpu.make_async_copy(tok_hbm, tok, load_sem.at[0])
    load_qry = pltpu.make_async_copy(qry_hbm, qry, load_sem.at[1])
    load_w = pltpu.make_async_copy(w_hbm.at[0], w, load_sem.at[2])
    load_tok.start()
    load_qry.start()
    load_w.start()

    r0, r1 = route_ref[0:1, :], route_ref[1:2, :]
    mem_row = lax.broadcasted_iota(jnp.int32, (MEMBERS, TOK), 0)
    hot0 = (mem_row == r0).astype(F32)
    hot1 = (mem_row == r1).astype(F32)
    ahead = (
        lax.broadcasted_iota(jnp.int32, (TOK, TOK), 0)
        < lax.broadcasted_iota(jnp.int32, (TOK, TOK), 1)
    ).astype(BF16)
    rank = mm((hot0 + hot1).astype(BF16), ahead)
    slot0 = r0 * CAP + jnp.sum(hot0 * rank, axis=0, keepdims=True).astype(jnp.int32)
    slot1 = r1 * CAP + jnp.sum(hot1 * rank, axis=0, keepdims=True).astype(jnp.int32)
    slot_row = lax.broadcasted_iota(jnp.int32, (ROWS, TOK), 0)
    is0, is1 = slot_row == slot0, slot_row == slot1
    onehot[...] = (is0.astype(F32) + is1.astype(F32)).astype(BF16)

    for r in range(3):

        @pl.when(tm < (1 << r))
        def _():
            srecv[r] = jnp.zeros((H, HD, HD), BF16)

    for d in range(1, BACK + 1):

        @pl.when(tm < d)
        def _():
            aprev[d - 1] = jnp.zeros((H, HD), F32)

    dec_wide = jnp.concatenate([dec_ref[...], jnp.zeros((128 - H, TOK), BF16)], axis=0)
    sendx[:, D:XW] = mm(onehot[...], dec_wide, 1, 1).astype(BF16)
    load_tok.wait()

    def gather_x(j, c):
        cols = pl.ds(pl.multiple_of(j * 256, 256), 256)
        sendx[:, cols] = mm(onehot[...], tok[:, cols]).astype(BF16)
        return c

    lax.fori_loop(0, D // 256, gather_x, 0)
    pl.semaphore_wait(barrier, PEERS + TM - 1)

    def x_copy(i, src, dst):
        return pltpu.make_async_remote_copy(
            src_ref=sendx.at[block(src)],
            dst_ref=recvx.at[block(dst)],
            send_sem=xs.at[i],
            recv_sem=xr.at[i],
            device_id=(tm, to[i]),
            device_id_type=MESH,
        )

    def q_copy(g, i, src, dst):
        return pltpu.make_async_remote_copy(
            src_ref=sendq.at[g, block(src)],
            dst_ref=recvq.at[g, block(dst)],
            send_sem=qs.at[g, i],
            recv_sem=qr.at[g, i],
            device_id=(tm, to[i]),
            device_id_type=MESH,
        )

    def o_copy(g, i, src, dst):
        return pltpu.make_async_remote_copy(
            src_ref=osend.at[g, block(src)],
            dst_ref=ret.at[g, block(dst)],
            send_sem=os_.at[g, i],
            recv_sem=or_.at[g, i],
            device_id=(tm, to[i]),
            device_id_type=MESH,
        )

    def a_copy(d):
        return pltpu.make_async_remote_copy(
            src_ref=atot,
            dst_ref=aprev.at[d - 1],
            send_sem=as_.at[d - 1],
            recv_sem=ar.at[d - 1],
            device_id=(lax.rem(tm + d, TM), me),
            device_id_type=MESH,
        )

    def s_copy(r, g):
        heads = pl.ds(g * GH, GH)
        return pltpu.make_async_remote_copy(
            src_ref=ssend.at[r, heads],
            dst_ref=srecv.at[r, heads],
            send_sem=ss.at[r, g],
            recv_sem=sr.at[r, g],
            device_id=(lax.rem(tm + (1 << r), TM), me),
            device_id_type=MESH,
        )

    for i in range(PEERS):
        x_copy(i, to[i], me).start()

    load_qry.wait()

    def gather_q(g, c):
        for half in range(GW // 256):
            cols = pl.ds(pl.multiple_of(g * GW + half * 256, 256), 256)
            sendq[g, :, half * 256 : half * 256 + 256] = mm(onehot[...], qry[:, cols]).astype(BF16)
        for i in range(PEERS):
            q_copy(g, i, to[i], me).start()
        recvq[g, block(me), :] = sendq[g, block(me), :]
        return c

    lax.fori_loop(0, GROUPS, gather_q, 0)
    recvx[block(me), :] = sendx[block(me), :]

    gates = jnp.where(is0, gate_ref[0:1, :], 0.0) + jnp.where(is1, gate_ref[1:2, :], 0.0)
    gates_hi = gates.astype(BF16)
    chi[...] = gates_hi.T
    clo[...] = (gates - gates_hi.astype(F32)).astype(BF16).T

    load_w.wait()
    for i in range(PEERS):
        x_copy(i, to[i], source[i]).wait_recv()

    tri_r = lax.broadcasted_iota(jnp.int32, (CHUNK, CHUNK), 0)
    tri_c = lax.broadcasted_iota(jnp.int32, (CHUNK, CHUNK), 1)
    lower = (tri_r >= tri_c).astype(BF16)
    total = jnp.zeros((H, HD), F32)
    for c in range(CHUNKS):
        logs = recvx[c * CHUNK : (c + 1) * CHUNK, D:XW]
        rcol[c] = mm(lower, logs)
        rows = mm(logs, lower, 0, 1)[:H]
        rrow[c] = rows
        end = jnp.broadcast_to(rows[:, CHUNK - 1 : CHUNK], (H, HD))
        ends[c] = end
        total = total + end
    atot[...] = total
    for d in range(1, BACK + 1):

        @pl.when(tm + d < TM)
        def _():
            a_copy(d).start()

    lane = lax.broadcasted_iota(jnp.int32, (CHUNK, HD), 1)

    def column(c, h):
        return jnp.sum(jnp.where(lane == h, rcol[c], 0.0), axis=1, keepdims=True)

    def project(j, carry):
        kcols = pl.ds(pl.multiple_of(j * 256, 256), 256)
        vcols = pl.ds(pl.multiple_of(D + j * 256, 256), 256)
        kb[j] = mm(recvx[:, :D], w[:, kcols]).astype(BF16)
        vb[j] = mm(recvx[:, :D], w[:, vcols]).astype(BF16)
        for hh in range(2):
            h = 2 * j + hh
            lanes = slice(hh * HD, hh * HD + HD)
            local = None
            for c in range(CHUNKS):
                rows = slice(c * CHUNK, (c + 1) * CHUNK)
                end = ends[c, pl.ds(h, 1), :]
                fade = jnp.exp(end - column(c, h))
                keys = (kb[j, rows, lanes].astype(F32) * fade).astype(BF16)
                part = mm(keys, vb[j, rows, lanes], 0, 0)
                if c < CHUNKS - 1:
                    ub[c, h] = part
                local = part if c == 0 else jnp.exp(end) * local + part
            inc[h] = local
            ssend[0, h] = local.astype(BF16)
        return carry

    def gain(h, first, last):
        span = aprev[first, pl.ds(h, 1), :]
        for d in range(first + 1, last):
            span = span + aprev[d, pl.ds(h, 1), :]
        return span

    def round0(h, carry):
        got = srecv[0, h].astype(F32)
        exc[h] = got
        new = jnp.exp(atot[pl.ds(h, 1), :]) * got + inc[h]
        inc[h] = new
        ssend[1, h] = new.astype(BF16)
        return carry

    def round1(h, carry):
        got = srecv[1, h].astype(F32)
        before = gain(h, 0, 1)
        exc[h] = jnp.exp(before) * got + exc[h]
        new = jnp.exp(before + atot[pl.ds(h, 1), :]) * got + inc[h]
        ssend[2, h] = new.astype(BF16)
        return carry

    def round2(h, carry):
        got = srecv[2, h].astype(F32)
        exc[h] = jnp.exp(gain(h, 0, 3)) * got + exc[h]
        return carry

    def send_state(r, g):
        @pl.when(tm + (1 << r) < TM)
        def _():
            s_copy(r, g).start()

    def take_state(r, g):
        @pl.when(tm >= (1 << r))
        def _():
            s_copy(r, g).wait_recv()

    def stage(s, carry):
        @pl.when(s < GROUPS)
        def _():
            lax.fori_loop(s * GP, (s + 1) * GP, project, 0)
            send_state(0, s)

        @pl.when(s == 0)
        def _():
            for d in range(1, BACK + 1):

                @pl.when(tm >= d)
                def _():
                    a_copy(d).wait_recv()

        for r, step in enumerate((round0, round1, round2)):
            g = s - 1 - r

            @pl.when(jnp.logical_and(g >= 0, g < GROUPS))
            def _():
                take_state(r, g)
                lax.fori_loop(g * GH, (g + 1) * GH, step, 0)
                if r < 2:
                    send_state(r + 1, g)

        return carry

    lax.fori_loop(0, GROUPS + 3, stage, 0)

    def emit(g, carry):
        for i in range(PEERS):
            q_copy(g, i, to[i], source[i]).wait_recv()

        def head(hh, inner):
            h = g * GH + hh
            j = lax.div(h, 2)
            klanes = pl.ds(pl.multiple_of(lax.rem(h, 2) * HD, HD), HD)
            qlanes = pl.ds(pl.multiple_of(hh * HD, HD), HD)
            state = exc[h]
            for c in range(CHUNKS):
                rows = slice(c * CHUNK, (c + 1) * CHUNK)
                q = recvq[g, rows, qlanes]
                k = kb[j, rows, klanes]
                v = vb[j, rows, klanes]
                col = column(c, h)
                spread = jnp.exp(jnp.minimum(col - rrow[c, pl.ds(h, 1), :], 0.0))
                scores = jnp.where(tri_r >= tri_c, mm(q, k, 1, 1) * spread, 0.0)
                o = mm(scores.astype(BF16), v) + mm(q, state.astype(BF16)) * jnp.exp(col)
                scale = lax.rsqrt(jnp.mean(o * o, axis=1, keepdims=True) + 1e-06)
                osend[g, rows, qlanes] = (o * scale).astype(BF16)
                if c < CHUNKS - 1:
                    state = jnp.exp(ends[c, pl.ds(h, 1), :]) * state + ub[c, h]
            return inner

        lax.fori_loop(0, GH, head, 0)
        for i in range(PEERS):
            o_copy(g, i, to[i], me).start()
        ret[g, block(me), :] = osend[g, block(me), :]
        return carry

    lax.fori_loop(0, GROUPS, emit, 0)

    def out_copy(g):
        cols = pl.ds(pl.multiple_of(g * GW, GW), GW)
        return pltpu.make_async_copy(outb.at[:, cols], out_hbm.at[:, cols], out_sem.at[g])

    def finish(g, carry):
        for i in range(PEERS):
            o_copy(g, i, to[i], source[i]).wait_recv()
        for half in range(GW // 256):
            cols = slice(half * 256, half * 256 + 256)
            where = pl.ds(pl.multiple_of(g * GW + half * 256, 256), 256)
            got = ret[g, :, cols]
            outb[:, where] = (mm(chi[...], got) + mm(clo[...], got)).astype(BF16)
        out_copy(g).start()
        return carry

    lax.fori_loop(0, GROUPS, finish, 0)

    for i in range(PEERS):
        x_copy(i, to[i], me).wait_send()

    def sent(g, carry):
        for i in range(PEERS):
            q_copy(g, i, to[i], me).wait_send()
            o_copy(g, i, to[i], me).wait_send()
        for r in range(3):

            @pl.when(tm + (1 << r) < TM)
            def _():
                s_copy(r, g).wait_send()

        out_copy(g).wait()
        return carry

    lax.fori_loop(0, GROUPS, sent, 0)
    for d in range(1, BACK + 1):

        @pl.when(tm + d < TM)
        def _():
            a_copy(d).wait_send()


def on_device(tokens, queries, log_decay, route_ids, gate_weights, kv_weight):
    anywhere = pl.BlockSpec(memory_space=pl.ANY)
    near = pl.BlockSpec(memory_space=pltpu.VMEM)
    dma = pltpu.SemaphoreType.DMA
    return pl.pallas_call(
        kernel,
        out_shape=jax.ShapeDtypeStruct((TOK, D), BF16),
        in_specs=[anywhere, anywhere, near, near, near, anywhere],
        out_specs=anywhere,
        scratch_shapes=[
            pltpu.VMEM((TOK, D), BF16),
            pltpu.VMEM((TOK, D), BF16),
            pltpu.VMEM((D, 2 * D), BF16),
            pltpu.VMEM((ROWS, TOK), BF16),
            pltpu.VMEM((TOK, ROWS), BF16),
            pltpu.VMEM((TOK, ROWS), BF16),
            pltpu.VMEM((ROWS, XW), BF16),
            pltpu.VMEM((ROWS, XW), BF16),
            pltpu.VMEM((GROUPS, ROWS, GW), BF16),
            pltpu.VMEM((GROUPS, ROWS, GW), BF16),
            pltpu.VMEM((PAIRS, ROWS, 256), BF16),
            pltpu.VMEM((PAIRS, ROWS, 256), BF16),
            pltpu.VMEM((GROUPS, ROWS, GW), BF16),
            pltpu.VMEM((GROUPS, ROWS, GW), BF16),
            pltpu.VMEM((TOK, D), BF16),
            pltpu.VMEM((CHUNKS, CHUNK, HD), F32),
            pltpu.VMEM((CHUNKS, H, CHUNK), F32),
            pltpu.VMEM((CHUNKS, H, HD), F32),
            pltpu.VMEM((H, HD), F32),
            pltpu.VMEM((BACK, H, HD), F32),
            pltpu.VMEM((CHUNKS - 1, H, HD, HD), F32),
            pltpu.VMEM((H, HD, HD), F32),
            pltpu.VMEM((H, HD, HD), F32),
            pltpu.VMEM((3, H, HD, HD), BF16),
            pltpu.VMEM((3, H, HD, HD), BF16),
            dma((3,)),
            dma((PEERS,)),
            dma((PEERS,)),
            dma((GROUPS, PEERS)),
            dma((GROUPS, PEERS)),
            dma((GROUPS, PEERS)),
            dma((GROUPS, PEERS)),
            dma((BACK,)),
            dma((BACK,)),
            dma((3, GROUPS)),
            dma((3, GROUPS)),
            dma((GROUPS,)),
        ],
        compiler_params=pltpu.CompilerParams(
            collective_id=0, has_side_effects=True, vmem_limit_bytes=60 * 2**20
        ),
        name="memories",
    )(tokens, queries, log_decay.T, route_ids.T, gate_weights.T, kv_weight)


def solution(mesh):
    rows = P(("tm", "mem"), None)
    return jax.shard_map(
        on_device,
        mesh=mesh,
        in_specs=(rows, rows, rows, rows, rows, P("mem", None, None)),
        out_specs=rows,
        check_vma=False,
    )
```

time: 337 us -> 135 us (0.40)
  the two profiles are of different devices: /device:TPU:87 before, /device:TPU:4 now
where the time goes in v1:
time: 135 us; the launch traced here: 134 us
  Pallas kernels  132 us (98%)
  local copies, waits for them, and re-layouts  2.3 us (2%)
    pallas_call x1, Pallas kernels, on_device(): pl.pallas_call(kernel, out_shape=jax.ShapeDtypeStruct((TOK, D), BF16), in...  132 us

profile of v1, /device:TPU:4, one launch (start us, length us, event | category | flops | bytes accessed | tf_op | source)
XLA Modules:
  0.0 133.9 jit_solution(14008152790111506876)
XLA Ops:
  0.0 131.6 %memories.1 = bf16[256,2048]{1,0:T(8,128)(2,1)} custom-call(bf16[256,2048]{1,0:T(8,128)(2,1)} %tok_hbm.1, bf16[256,2048]{1,0:T(8,128)(2,1)} %qry_hbm.1, bf16[16,256]{1,0:T(8,128)(2,1)} %bitcast.3, s32[2,256]{1,0:T(2,128)} %bitcast.4, f32[2,256]{1,0:T(2,128)} %bitcast.5, bf16[1,2048,4096]{2,1,0:T(8,128)(2,1)} %w_hbm.1), custom_call_target="tpu_custom_call" | custom-call | tf_op jit(solution)/shard_map/memories/pallas_call | solution.py:385
  131.6 2.3 %copy.8 = bf16[256,2048]{1,0:T(8,128)(2,1)} copy(bf16[256,2048]{1,0:T(8,128)(2,1)} %memories.1) | data formatting | bytes 2097152

commit v2 on v1

--- a/solution.py
+++ b/solution.py
@@ -29,10 +29,9 @@
 GP = PAIRS // GROUPS
 
 SHIFTS = (
-    (1, 0), (3, 0), (0, 1), (0, 3),
-    (1, 1), (3, 3), (1, 3), (3, 1),
-    (2, 1), (2, 3), (1, 2), (3, 2),
-    (2, 0), (0, 2), (2, 2),
+    (2, 2), (0, 2), (2, 0), (3, 2), (1, 2),
+    (2, 3), (2, 1), (3, 1), (1, 3), (3, 3),
+    (3, 0), (0, 3), (0, 1), (1, 1), (1, 0),
 )
 PEERS = len(SHIFTS)
 BACK = 3
@@ -56,8 +55,10 @@
     def at(dy, dz):
         return lax.rem(my + dy, MEM_Y) * MEM_Z + lax.rem(mz + dz, MEM_Z)
 
-    to = [at(dy, dz) for dy, dz in SHIFTS]
-    source = [at(MEM_Y - dy, MEM_Z - dz) for dy, dz in SHIFTS]
+    core = lax.rem(tm, 2)
+    turned = [(dy + core * (dz - dy), dz + core * (dy - dz)) for dy, dz in SHIFTS]
+    to = [at(dy, dz) for dy, dz in turned]
+    source = [at(MEM_Y - dy, MEM_Z - dz) for dy, dz in turned]
 
     def block(place):
         return pl.ds(pl.multiple_of(place * CAP, 16), CAP)

time: 135 us -> 130 us (0.963)
  Pallas kernels: 132 us -> 127 us
    pallas_call x1, Pallas kernels: 132 us -> 127 us  [on_device(): pl.pallas_call(kernel, out_shape=jax.ShapeDtypeStruct((TOK, D), BF16), in...]
where the time goes in v2:
time: 130 us; the launch traced here: 129 us
  Pallas kernels  127 us (98%)
  local copies, waits for them, and re-layouts  2.3 us (2%)
    pallas_call x1, Pallas kernels, on_device(): pl.pallas_call(kernel, out_shape=jax.ShapeDtypeStruct((TOK, D), BF16), in...  127 us

profile of v2, /device:TPU:4, one launch (start us, length us, event | category | flops | bytes accessed | tf_op | source)
XLA Modules:
  0.0 129.3 jit_solution(3069021542411373863)
XLA Ops:
  0.0 127.0 %memories.1 = bf16[256,2048]{1,0:T(8,128)(2,1)} custom-call(bf16[256,2048]{1,0:T(8,128)(2,1)} %tok_hbm.1, bf16[256,2048]{1,0:T(8,128)(2,1)} %qry_hbm.1, bf16[16,256]{1,0:T(8,128)(2,1)} %bitcast.3, s32[2,256]{1,0:T(2,128)} %bitcast.4, f32[2,256]{1,0:T(2,128)} %bitcast.5, bf16[1,2048,4096]{2,1,0:T(8,128)(2,1)} %w_hbm.1), custom_call_target="tpu_custom_call" | custom-call | tf_op jit(solution)/shard_map/memories/pallas_call | solution.py:386
  127.0 2.3 %copy.8 = bf16[256,2048]{1,0:T(8,128)(2,1)} copy(bf16[256,2048]{1,0:T(8,128)(2,1)} %memories.1) | data formatting | bytes 2097152

commit v3 on v2

--- a/solution.py
+++ b/solution.py
@@ -41,6 +41,11 @@
     return lax.dot_general(a, b, (((da,), (db,)), ((), ())), preferred_element_type=F32)
 
 
+def split(a):
+    high = a.astype(BF16)
+    return high, (a - high.astype(F32)).astype(BF16)
+
+
 def kernel(
     tok_hbm, qry_hbm, dec_ref, route_ref, gate_ref, w_hbm, out_hbm,
     tok, qry, w, onehot, chi, clo,
@@ -58,10 +63,14 @@
     core = lax.rem(tm, 2)
     turned = [(dy + core * (dz - dy), dz + core * (dy - dz)) for dy, dz in SHIFTS]
     to = [at(dy, dz) for dy, dz in turned]
-    source = [at(MEM_Y - dy, MEM_Z - dz) for dy, dz in turned]
 
     def block(place):
         return pl.ds(pl.multiple_of(place * CAP, 16), CAP)
+
+    load_tok = pltpu.make_async_copy(tok_hbm, tok, load_sem.at[0])
+    load_qry = pltpu.make_async_copy(qry_hbm, qry, load_sem.at[1])
+    load_w = pltpu.make_async_copy(w_hbm.at[0], w, load_sem.at[2])
+    load_tok.start()
 
     barrier = pltpu.get_barrier_semaphore()
     for i in range(PEERS):
@@ -70,13 +79,6 @@
         pl.semaphore_signal(
             barrier, inc=1, device_id=(lax.rem(tm + d, TM), me), device_id_type=MESH
         )
-
-    load_tok = pltpu.make_async_copy(tok_hbm, tok, load_sem.at[0])
-    load_qry = pltpu.make_async_copy(qry_hbm, qry, load_sem.at[1])
-    load_w = pltpu.make_async_copy(w_hbm.at[0], w, load_sem.at[2])
-    load_tok.start()
-    load_qry.start()
-    load_w.start()
 
     r0, r1 = route_ref[0:1, :], route_ref[1:2, :]
     mem_row = lax.broadcasted_iota(jnp.int32, (MEMBERS, TOK), 0)
@@ -93,59 +95,39 @@
     is0, is1 = slot_row == slot0, slot_row == slot1
     onehot[...] = (is0.astype(F32) + is1.astype(F32)).astype(BF16)
 
-    for r in range(3):
-
-        @pl.when(tm < (1 << r))
-        def _():
-            srecv[r] = jnp.zeros((H, HD, HD), BF16)
-
-    for d in range(1, BACK + 1):
-
-        @pl.when(tm < d)
-        def _():
-            aprev[d - 1] = jnp.zeros((H, HD), F32)
-
     dec_wide = jnp.concatenate([dec_ref[...], jnp.zeros((128 - H, TOK), BF16)], axis=0)
     sendx[:, D:XW] = mm(onehot[...], dec_wide, 1, 1).astype(BF16)
-    load_tok.wait()
-
-    def gather_x(j, c):
-        cols = pl.ds(pl.multiple_of(j * 256, 256), 256)
-        sendx[:, cols] = mm(onehot[...], tok[:, cols]).astype(BF16)
-        return c
-
-    lax.fori_loop(0, D // 256, gather_x, 0)
-    pl.semaphore_wait(barrier, PEERS + TM - 1)
-
     def x_copy(i, src, dst):
         return pltpu.make_async_remote_copy(
-            src_ref=sendx.at[block(src)],
-            dst_ref=recvx.at[block(dst)],
-            send_sem=xs.at[i],
-            recv_sem=xr.at[i],
+            src_ref=sendx.at[src],
+            dst_ref=recvx.at[dst],
+            send_sem=xs.at[0],
+            recv_sem=xr.at[0],
             device_id=(tm, to[i]),
             device_id_type=MESH,
         )
 
     def q_copy(g, i, src, dst):
         return pltpu.make_async_remote_copy(
-            src_ref=sendq.at[g, block(src)],
-            dst_ref=recvq.at[g, block(dst)],
-            send_sem=qs.at[g, i],
-            recv_sem=qr.at[g, i],
+            src_ref=sendq.at[g, src],
+            dst_ref=recvq.at[g, dst],
+            send_sem=qs.at[g],
+            recv_sem=qr.at[g],
             device_id=(tm, to[i]),
             device_id_type=MESH,
         )
 
     def o_copy(g, i, src, dst):
         return pltpu.make_async_remote_copy(
-            src_ref=osend.at[g, block(src)],
-            dst_ref=ret.at[g, block(dst)],
-            send_sem=os_.at[g, i],
-            recv_sem=or_.at[g, i],
+            src_ref=osend.at[g, src],
+            dst_ref=ret.at[g, dst],
+            send_sem=os_.at[g],
+            recv_sem=or_.at[g],
             device_id=(tm, to[i]),
             device_id_type=MESH,
         )
+
+    every = slice(0, PEERS * CAP)
 
     def a_copy(d):
         return pltpu.make_async_remote_copy(
@@ -168,8 +150,29 @@
             device_id_type=MESH,
         )
 
+    load_tok.wait()
+    pl.semaphore_wait(barrier, PEERS + TM - 1)
     for i in range(PEERS):
-        x_copy(i, to[i], me).start()
+        rows = block(to[i])
+        sendx[rows, :D] = mm(onehot[rows, :], tok[...]).astype(BF16)
+        x_copy(i, rows, block(me)).start()
+    load_qry.start()
+    load_w.start()
+    mine = block(me)
+    recvx[mine, :D] = mm(onehot[mine, :], tok[...]).astype(BF16)
+    recvx[mine, D:XW] = sendx[mine, D:XW]
+
+    for r in range(3):
+
+        @pl.when(tm < (1 << r))
+        def _():
+            srecv[r] = jnp.zeros((H, HD, HD), BF16)
+
+    for d in range(1, BACK + 1):
+
+        @pl.when(tm < d)
+        def _():
+            aprev[d - 1] = jnp.zeros((H, HD), F32)
 
     load_qry.wait()
 
@@ -178,21 +181,19 @@
             cols = pl.ds(pl.multiple_of(g * GW + half * 256, 256), 256)
             sendq[g, :, half * 256 : half * 256 + 256] = mm(onehot[...], qry[:, cols]).astype(BF16)
         for i in range(PEERS):
-            q_copy(g, i, to[i], me).start()
-        recvq[g, block(me), :] = sendq[g, block(me), :]
+            q_copy(g, i, block(to[i]), mine).start()
+        recvq[g, mine, :] = sendq[g, mine, :]
         return c
 
     lax.fori_loop(0, GROUPS, gather_q, 0)
-    recvx[block(me), :] = sendx[block(me), :]
 
     gates = jnp.where(is0, gate_ref[0:1, :], 0.0) + jnp.where(is1, gate_ref[1:2, :], 0.0)
-    gates_hi = gates.astype(BF16)
+    gates_hi, gates_lo = split(gates)
     chi[...] = gates_hi.T
-    clo[...] = (gates - gates_hi.astype(F32)).astype(BF16).T
+    clo[...] = gates_lo.T
 
     load_w.wait()
-    for i in range(PEERS):
-        x_copy(i, to[i], source[i]).wait_recv()
+    x_copy(0, every, every).wait_recv()
 
     tri_r = lax.broadcasted_iota(jnp.int32, (CHUNK, CHUNK), 0)
     tri_c = lax.broadcasted_iota(jnp.int32, (CHUNK, CHUNK), 1)
@@ -277,37 +278,8 @@
         def _():
             s_copy(r, g).wait_recv()
 
-    def stage(s, carry):
-        @pl.when(s < GROUPS)
-        def _():
-            lax.fori_loop(s * GP, (s + 1) * GP, project, 0)
-            send_state(0, s)
-
-        @pl.when(s == 0)
-        def _():
-            for d in range(1, BACK + 1):
-
-                @pl.when(tm >= d)
-                def _():
-                    a_copy(d).wait_recv()
-
-        for r, step in enumerate((round0, round1, round2)):
-            g = s - 1 - r
-
-            @pl.when(jnp.logical_and(g >= 0, g < GROUPS))
-            def _():
-                take_state(r, g)
-                lax.fori_loop(g * GH, (g + 1) * GH, step, 0)
-                if r < 2:
-                    send_state(r + 1, g)
-
-        return carry
-
-    lax.fori_loop(0, GROUPS + 3, stage, 0)
-
-    def emit(g, carry):
-        for i in range(PEERS):
-            q_copy(g, i, to[i], source[i]).wait_recv()
+    def emit(g):
+        q_copy(g, 0, every, every).wait_recv()
 
         def head(hh, inner):
             h = g * GH + hh
@@ -323,7 +295,9 @@
                 col = column(c, h)
                 spread = jnp.exp(jnp.minimum(col - rrow[c, pl.ds(h, 1), :], 0.0))
                 scores = jnp.where(tri_r >= tri_c, mm(q, k, 1, 1) * spread, 0.0)
-                o = mm(scores.astype(BF16), v) + mm(q, state.astype(BF16)) * jnp.exp(col)
+                s_hi, s_lo = split(scores)
+                t_hi, t_lo = split(state)
+                o = mm(s_hi, v) + mm(s_lo, v) + (mm(q, t_hi) + mm(q, t_lo)) * jnp.exp(col)
                 scale = lax.rsqrt(jnp.mean(o * o, axis=1, keepdims=True) + 1e-06)
                 osend[g, rows, qlanes] = (o * scale).astype(BF16)
                 if c < CHUNKS - 1:
@@ -332,19 +306,46 @@
 
         lax.fori_loop(0, GH, head, 0)
         for i in range(PEERS):
-            o_copy(g, i, to[i], me).start()
-        ret[g, block(me), :] = osend[g, block(me), :]
-        return carry
-
-    lax.fori_loop(0, GROUPS, emit, 0)
+            o_copy(g, i, block(to[i]), mine).start()
+        ret[g, mine, :] = osend[g, mine, :]
+
+    def stage(s, carry):
+        @pl.when(s < GROUPS)
+        def _():
+            lax.fori_loop(s * GP, (s + 1) * GP, project, 0)
+            send_state(0, s)
+
+        @pl.when(s == 0)
+        def _():
+            for d in range(1, BACK + 1):
+
+                @pl.when(tm >= d)
+                def _():
+                    a_copy(d).wait_recv()
+
+        for r, step in enumerate((round0, round1, round2)):
+            g = s - 1 - r
+
+            @pl.when(jnp.logical_and(g >= 0, g < GROUPS))
+            def _():
+                take_state(r, g)
+                lax.fori_loop(g * GH, (g + 1) * GH, step, 0)
+                if r < 2:
+                    send_state(r + 1, g)
+                else:
+                    emit(g)
+
+        return carry
+
+    lax.fori_loop(0, GROUPS + 3, stage, 0)
+
 
     def out_copy(g):
         cols = pl.ds(pl.multiple_of(g * GW, GW), GW)
         return pltpu.make_async_copy(outb.at[:, cols], out_hbm.at[:, cols], out_sem.at[g])
 
     def finish(g, carry):
-        for i in range(PEERS):
-            o_copy(g, i, to[i], source[i]).wait_recv()
+        o_copy(g, 0, every, every).wait_recv()
         for half in range(GW // 256):
             cols = slice(half * 256, half * 256 + 256)
             where = pl.ds(pl.multiple_of(g * GW + half * 256, 256), 256)
@@ -355,13 +356,11 @@
 
     lax.fori_loop(0, GROUPS, finish, 0)
 
-    for i in range(PEERS):
-        x_copy(i, to[i], me).wait_send()
+    x_copy(0, every, every).wait_send()
 
     def sent(g, carry):
-        for i in range(PEERS):
-            q_copy(g, i, to[i], me).wait_send()
-            o_copy(g, i, to[i], me).wait_send()
+        q_copy(g, 0, every, every).wait_send()
+        o_copy(g, 0, every, every).wait_send()
         for r in range(3):
 
             @pl.when(tm + (1 << r) < TM)
@@ -415,12 +414,12 @@
             pltpu.VMEM((3, H, HD, HD), BF16),
             pltpu.VMEM((3, H, HD, HD), BF16),
             dma((3,)),
-            dma((PEERS,)),
-            dma((PEERS,)),
-            dma((GROUPS, PEERS)),
-            dma((GROUPS, PEERS)),
-            dma((GROUPS, PEERS)),
-            dma((GROUPS, PEERS)),
+            dma((1,)),
+            dma((1,)),
+            dma((GROUPS,)),
+            dma((GROUPS,)),
+            dma((GROUPS,)),
+            dma((GROUPS,)),
             dma((BACK,)),
             dma((BACK,)),
             dma((3, GROUPS)),

time: 130 us -> 121 us (0.931); the launches traced: 129 us -> 119 us
  Pallas kernels: 127 us -> 116 us
    pallas_call x1, Pallas kernels: 127 us -> 116 us  [on_device(): pl.pallas_call(kernel, out_shape=jax.ShapeDtypeStruct((TOK, D), BF16), in...]
where the time goes in v3:
time: 121 us; the launch traced here: 119 us
  Pallas kernels  116 us (96%)
  local copies, waits for them, and re-layouts  2.3 us (2%)
    pallas_call x1, Pallas kernels, on_device(): pl.pallas_call(kernel, out_shape=jax.ShapeDtypeStruct((TOK, D), BF16), in...  116 us

profile of v3, /device:TPU:4, one launch (start us, length us, event | category | flops | bytes accessed | tf_op | source)
XLA Modules:
  0.0 118.8 jit_solution(3290807054560647958)
XLA Ops:
  0.0 116.4 %memories.1 = bf16[256,2048]{1,0:T(8,128)(2,1)} custom-call(bf16[256,2048]{1,0:T(8,128)(2,1)} %tok_hbm.1, bf16[256,2048]{1,0:T(8,128)(2,1)} %qry_hbm.1, bf16[16,256]{1,0:T(8,128)(2,1)} %bitcast.3, s32[2,256]{1,0:T(2,128)} %bitcast.4, f32[2,256]{1,0:T(2,128)} %bitcast.5, bf16[1,2048,4096]{2,1,0:T(8,128)(2,1)} %w_hbm.1), custom_call_target="tpu_custom_call" | custom-call | tf_op jit(solution)/shard_map/memories/pallas_call | solution.py:385
  116.5 2.3 %copy.8 = bf16[256,2048]{1,0:T(8,128)(2,1)} copy(bf16[256,2048]{1,0:T(8,128)(2,1)} %memories.1) | data formatting | bytes 2097152

commit v4 on v3

--- a/solution.py
+++ b/solution.py
@@ -19,7 +19,6 @@
 D = 2048
 H = 16
 HD = 128
-XW = D + 128
 CHUNK = 256
 CHUNKS = ROWS // CHUNK
 GROUPS = 4
@@ -34,6 +33,11 @@
     (3, 0), (0, 3), (0, 1), (1, 1), (1, 0),
 )
 PEERS = len(SHIFTS)
+HALF_SHIFTS = ((1, 2), (0, 2), (1, 1), (1, 3), (0, 1), (0, 3), (1, 0))
+HALF = MEMBERS // 2
+HALF_PEERS = len(HALF_SHIFTS)
+QUARTERS = 4
+QW = D // QUARTERS
 BACK = 3
 
 
@@ -48,10 +52,11 @@
 
 def kernel(
     tok_hbm, qry_hbm, dec_ref, route_ref, gate_ref, w_hbm, out_hbm,
-    tok, qry, w, onehot, chi, clo,
-    sendx, recvx, sendq, recvq, kb, vb, osend, ret, outb,
+    tok, qry, w, onehot, picks, chi, clo, slots, slotp, xp, qp,
+    sendd, recvd, sendx, recvx, sendq, recvq, kb, vb, osend, ret, outb,
     rcol, rrow, ends, atot, aprev, ub, inc, exc, ssend, srecv,
-    load_sem, xs, xr, qs, qr, os_, or_, as_, ar, ss, sr, out_sem,
+    load_sem, sps, spr, xps, xpr, qps, qpr, ds_, dr,
+    xs, xr, qs, qr, os_, or_, as_, ar, ss, sr, out_sem,
 ):
     tm = lax.axis_index("tm")
     me = lax.axis_index("mem")
@@ -64,6 +69,23 @@
     turned = [(dy + core * (dz - dy), dz + core * (dy - dz)) for dy, dz in SHIFTS]
     to = [at(dy, dz) for dy, dz in turned]
 
+    y_swap, y_flip = my + 1 - 2 * lax.rem(my, 2), MEM_Y - 1 - my
+    z_swap, z_flip = mz + 1 - 2 * lax.rem(mz, 2), MEM_Z - 1 - mz
+    partner = (
+        y_swap * MEM_Z + mz,
+        y_flip * MEM_Z + mz,
+        my * MEM_Z + z_swap,
+        my * MEM_Z + z_flip,
+    )
+    other = (y_flip, y_swap, z_flip, z_swap)
+
+    def in_half(g, across, step):
+        if g < 2:
+            ring = lax.rem(mz + step, MEM_Z)
+            return (other[g] if across else my) * MEM_Z + ring, across * 4 + ring
+        ring = lax.rem(my + step, MEM_Y)
+        return ring * MEM_Z + (other[g] if across else mz), across * 4 + ring
+
     def block(place):
         return pl.ds(pl.multiple_of(place * CAP, 16), CAP)
 
@@ -71,6 +93,7 @@
     load_qry = pltpu.make_async_copy(qry_hbm, qry, load_sem.at[1])
     load_w = pltpu.make_async_copy(w_hbm.at[0], w, load_sem.at[2])
     load_tok.start()
+    load_qry.start()
 
     barrier = pltpu.get_barrier_semaphore()
     for i in range(PEERS):
@@ -89,31 +112,86 @@
         < lax.broadcasted_iota(jnp.int32, (TOK, TOK), 1)
     ).astype(BF16)
     rank = mm((hot0 + hot1).astype(BF16), ahead)
-    slot0 = r0 * CAP + jnp.sum(hot0 * rank, axis=0, keepdims=True).astype(jnp.int32)
-    slot1 = r1 * CAP + jnp.sum(hot1 * rank, axis=0, keepdims=True).astype(jnp.int32)
-    slot_row = lax.broadcasted_iota(jnp.int32, (ROWS, TOK), 0)
+    slot0 = r0.astype(F32) * CAP + jnp.sum(hot0 * rank, axis=0, keepdims=True)
+    slot1 = r1.astype(F32) * CAP + jnp.sum(hot1 * rank, axis=0, keepdims=True)
+    slots[...] = jnp.concatenate([slot0, slot1, jnp.zeros((6, TOK), F32)], axis=0)
+    slot_row = lax.broadcasted_iota(jnp.int32, (ROWS + 128, TOK), 0).astype(F32)
     is0, is1 = slot_row == slot0, slot_row == slot1
     onehot[...] = (is0.astype(F32) + is1.astype(F32)).astype(BF16)
 
-    dec_wide = jnp.concatenate([dec_ref[...], jnp.zeros((128 - H, TOK), BF16)], axis=0)
-    sendx[:, D:XW] = mm(onehot[...], dec_wide, 1, 1).astype(BF16)
-    def x_copy(i, src, dst):
-        return pltpu.make_async_remote_copy(
-            src_ref=sendx.at[src],
-            dst_ref=recvx.at[dst],
-            send_sem=xs.at[0],
-            recv_sem=xr.at[0],
+    def gather_d(e, c):
+        rows = onehot[pl.ds(pl.multiple_of(e * CAP, 16), 128), :]
+        sendd[e] = mm(dec_ref[...], rows, 1, 1).astype(BF16)
+        return c
+
+    def slot_copy(g):
+        return pltpu.make_async_remote_copy(
+            src_ref=slots,
+            dst_ref=slotp.at[g],
+            send_sem=sps.at[0],
+            recv_sem=spr.at[g],
+            device_id=(tm, partner[g]),
+            device_id_type=MESH,
+        )
+
+    def xp_copy(g):
+        return pltpu.make_async_remote_copy(
+            src_ref=tok_hbm.at[:, g * QW : (g + 1) * QW],
+            dst_ref=xp.at[g],
+            send_sem=xps.at[0],
+            recv_sem=xpr.at[g],
+            device_id=(tm, partner[g]),
+            device_id_type=MESH,
+        )
+
+    def qp_copy(g, u):
+        first = (u * QUARTERS + g) * 256
+        return pltpu.make_async_remote_copy(
+            src_ref=qry_hbm.at[:, first : first + 256],
+            dst_ref=qp.at[g, u],
+            send_sem=qps.at[0],
+            recv_sem=qpr.at[g],
+            device_id=(tm, partner[g]),
+            device_id_type=MESH,
+        )
+
+    def whole(ref, send_sem, recv_sem):
+        return pltpu.make_async_remote_copy(
+            src_ref=ref,
+            dst_ref=ref,
+            send_sem=send_sem,
+            recv_sem=recv_sem,
+            device_id=(tm, to[0]),
+            device_id_type=MESH,
+        )
+
+    def d_copy(i):
+        return pltpu.make_async_remote_copy(
+            src_ref=sendd.at[to[i]],
+            dst_ref=recvd.at[me],
+            send_sem=ds_.at[0],
+            recv_sem=dr.at[0],
             device_id=(tm, to[i]),
             device_id_type=MESH,
         )
 
-    def q_copy(g, i, src, dst):
-        return pltpu.make_async_remote_copy(
-            src_ref=sendq.at[g, src],
-            dst_ref=recvq.at[g, dst],
-            send_sem=qs.at[g],
-            recv_sem=qr.at[g],
-            device_id=(tm, to[i]),
+    def x_copy(g, own, src, dst, place):
+        return pltpu.make_async_remote_copy(
+            src_ref=sendx.at[g, own, src],
+            dst_ref=recvx.at[dst, g * QW : (g + 1) * QW],
+            send_sem=xs.at[g],
+            recv_sem=xr.at[g],
+            device_id=(tm, place),
+            device_id_type=MESH,
+        )
+
+    def q_copy(j, own, src, dst, place):
+        return pltpu.make_async_remote_copy(
+            src_ref=sendq.at[j, own, src],
+            dst_ref=recvq.at[j, dst],
+            send_sem=qs.at[j],
+            recv_sem=qr.at[j],
+            device_id=(tm, place),
             device_id_type=MESH,
         )
 
@@ -128,6 +206,7 @@
         )
 
     every = slice(0, PEERS * CAP)
+    half_every = slice(0, 2 * HALF_PEERS * CAP)
 
     def a_copy(d):
         return pltpu.make_async_remote_copy(
@@ -144,23 +223,90 @@
         return pltpu.make_async_remote_copy(
             src_ref=ssend.at[r, heads],
             dst_ref=srecv.at[r, heads],
-            send_sem=ss.at[r, g],
+            send_sem=ss.at[r],
             recv_sem=sr.at[r, g],
             device_id=(lax.rem(tm + (1 << r), TM), me),
             device_id_type=MESH,
         )
 
+    pl.semaphore_wait(barrier, PEERS + TM - 1)
+    for g in range(QUARTERS):
+        slot_copy(g).start()
+    for g in range(QUARTERS):
+        xp_copy(g).start()
+    lax.fori_loop(0, MEMBERS, gather_d, 0)
+    for i in range(PEERS):
+        d_copy(i).start()
+    for u in range(2):
+        for g in range(QUARTERS):
+            qp_copy(g, u).start()
+    recvd[me] = sendd[me]
+
+    pick_row = lax.broadcasted_iota(jnp.int32, (HALF * CAP, TOK), 0)
+    over = (pick_row >= HALF * CAP // 2).astype(jnp.int32)
+    ring_row = pick_row - over * (HALF * CAP // 2)
+    ring = sum((ring_row >= k * CAP).astype(jnp.int32) for k in range(1, 4))
+
+    def wanted(g):
+        if g < 2:
+            return (ring_row + (my + over * (other[g] - my)) * (MEM_Z * CAP)).astype(F32)
+        column_slot = (mz + over * (other[g] - mz)) * CAP
+        return (ring_row + ring * ((MEM_Z - 1) * CAP) + column_slot).astype(F32)
+
+    def pick(g, slots_now):
+        goal = wanted(g)
+        first, second = goal == slots_now[0:1, :], goal == slots_now[1:2, :]
+        return (first.astype(F32) + second.astype(F32)).astype(BF16)
+
     load_tok.wait()
-    pl.semaphore_wait(barrier, PEERS + TM - 1)
-    for i in range(PEERS):
-        rows = block(to[i])
-        sendx[rows, :D] = mm(onehot[rows, :], tok[...]).astype(BF16)
-        x_copy(i, rows, block(me)).start()
-    load_qry.start()
+    for g in range(QUARTERS):
+        picks[g, 0] = pick(g, slots[...])
+        sendx[g, 0] = mm(picks[g, 0], tok[:, g * QW : (g + 1) * QW]).astype(BF16)
+    for g in range(QUARTERS):
+        slot_copy(g).wait_recv()
+        picks[g, 1] = pick(g, slotp[g])
+    for g in range(QUARTERS):
+        whole(xp.at[g], xps.at[0], xpr.at[g]).wait_recv()
+        sendx[g, 1] = mm(picks[g, 1], xp[g]).astype(BF16)
+    mine = block(me)
+    for across, step in HALF_SHIFTS:
+        for g in range(QUARTERS):
+            place, number = in_half(g, across, step)
+            for own in range(2):
+                dst = block(partner[g]) if own else mine
+                x_copy(g, own, block(number), dst, place).start()
     load_w.start()
-    mine = block(me)
-    recvx[mine, :D] = mm(onehot[mine, :], tok[...]).astype(BF16)
-    recvx[mine, D:XW] = sendx[mine, D:XW]
+    for g in range(QUARTERS):
+        number = in_half(g, 0, 0)[1]
+        cols = slice(g * QW, (g + 1) * QW)
+        recvx[mine, cols] = sendx[g, 0, block(number), :]
+        recvx[block(partner[g]), cols] = sendx[g, 1, block(number), :]
+
+    load_qry.wait()
+    for g in range(QUARTERS):
+        whole(qp.at[g], qps.at[0], qpr.at[g]).wait_recv()
+
+    def gather_q(u, c):
+        for g in range(QUARTERS):
+            j = u * QUARTERS + g
+            cols = pl.ds(pl.multiple_of(j * 256, 256), 256)
+            sendq[j, 0] = mm(picks[g, 0], qry[:, cols]).astype(BF16)
+            sendq[j, 1] = mm(picks[g, 1], qp[g, u]).astype(BF16)
+        for across, step in HALF_SHIFTS:
+            for g in range(QUARTERS):
+                place, number = in_half(g, across, step)
+                j = u * QUARTERS + g
+                for own in range(2):
+                    dst = block(partner[g]) if own else mine
+                    q_copy(j, own, block(number), dst, place).start()
+        for g in range(QUARTERS):
+            j = u * QUARTERS + g
+            number = in_half(g, 0, 0)[1]
+            recvq[j, mine, :] = sendq[j, 0, block(number), :]
+            recvq[j, block(partner[g]), :] = sendq[j, 1, block(number), :]
+        return c
+
+    lax.fori_loop(0, 2, gather_q, 0)
 
     for r in range(3):
 
@@ -174,36 +320,36 @@
         def _():
             aprev[d - 1] = jnp.zeros((H, HD), F32)
 
-    load_qry.wait()
-
-    def gather_q(g, c):
-        for half in range(GW // 256):
-            cols = pl.ds(pl.multiple_of(g * GW + half * 256, 256), 256)
-            sendq[g, :, half * 256 : half * 256 + 256] = mm(onehot[...], qry[:, cols]).astype(BF16)
-        for i in range(PEERS):
-            q_copy(g, i, block(to[i]), mine).start()
-        recvq[g, mine, :] = sendq[g, mine, :]
-        return c
-
-    lax.fori_loop(0, GROUPS, gather_q, 0)
-
     gates = jnp.where(is0, gate_ref[0:1, :], 0.0) + jnp.where(is1, gate_ref[1:2, :], 0.0)
+    gates = gates[:ROWS]
     gates_hi, gates_lo = split(gates)
     chi[...] = gates_hi.T
     clo[...] = gates_lo.T
 
-    load_w.wait()
-    x_copy(0, every, every).wait_recv()
-
+    whole(recvd.at[0:PEERS], ds_.at[0], dr.at[0]).wait_recv()
     tri_r = lax.broadcasted_iota(jnp.int32, (CHUNK, CHUNK), 0)
     tri_c = lax.broadcasted_iota(jnp.int32, (CHUNK, CHUNK), 1)
-    lower = (tri_r >= tri_c).astype(BF16)
+    place_row = lax.broadcasted_iota(jnp.int32, (128, CHUNK), 0)
+    place_col = lax.broadcasted_iota(jnp.int32, (128, CHUNK), 1)
+    used = place_row < CAP
+
+    def add_logs(src, sums):
+        at_row = place_row + src * CAP
+        out = []
+        for c in range(CHUNKS):
+            within = jnp.logical_and(at_row >= c * CHUNK, at_row <= place_col + c * CHUNK)
+            take = jnp.where(jnp.logical_and(used, within), 1.0, 0.0).astype(BF16)
+            out.append(sums[c] + mm(recvd[src], take))
+        return tuple(out)
+
+    sums = lax.fori_loop(
+        0, MEMBERS, add_logs, tuple(jnp.zeros((H, CHUNK), F32) for c in range(CHUNKS))
+    )
     total = jnp.zeros((H, HD), F32)
     for c in range(CHUNKS):
-        logs = recvx[c * CHUNK : (c + 1) * CHUNK, D:XW]
-        rcol[c] = mm(lower, logs)
-        rows = mm(logs, lower, 0, 1)[:H]
+        rows = sums[c]
         rrow[c] = rows
+        rcol[c] = jnp.concatenate([rows, jnp.zeros((HD - H, CHUNK), F32)], axis=0).T
         end = jnp.broadcast_to(rows[:, CHUNK - 1 : CHUNK], (H, HD))
         ends[c] = end
         total = total + end
@@ -214,16 +360,22 @@
         def _():
             a_copy(d).start()
 
+    load_w.wait()
+    for g in range(QUARTERS):
+        x_copy(g, 0, slice(0, CAP), half_every, to[0]).wait_recv()
+
     lane = lax.broadcasted_iota(jnp.int32, (CHUNK, HD), 1)
 
     def column(c, h):
         return jnp.sum(jnp.where(lane == h, rcol[c], 0.0), axis=1, keepdims=True)
 
     def project(j, carry):
-        kcols = pl.ds(pl.multiple_of(j * 256, 256), 256)
-        vcols = pl.ds(pl.multiple_of(D + j * 256, 256), 256)
-        kb[j] = mm(recvx[:, :D], w[:, kcols]).astype(BF16)
-        vb[j] = mm(recvx[:, :D], w[:, vcols]).astype(BF16)
+        def columns(first):
+            cols = pl.ds(pl.multiple_of(first, 256), 256)
+            return mm(recvx[...], w[:, cols]).astype(BF16)
+
+        kb[j] = columns(j * 256)
+        vb[j] = columns(D + j * 256)
         for hh in range(2):
             h = 2 * j + hh
             lanes = slice(hh * HD, hh * HD + HD)
@@ -279,7 +431,8 @@
             s_copy(r, g).wait_recv()
 
     def emit(g):
-        q_copy(g, 0, every, every).wait_recv()
+        for p in range(2):
+            q_copy(2 * g + p, 0, slice(0, CAP), half_every, to[0]).wait_recv()
 
         def head(hh, inner):
             h = g * GH + hh
@@ -289,7 +442,7 @@
             state = exc[h]
             for c in range(CHUNKS):
                 rows = slice(c * CHUNK, (c + 1) * CHUNK)
-                q = recvq[g, rows, qlanes]
+                q = recvq[j, rows, klanes]
                 k = kb[j, rows, klanes]
                 v = vb[j, rows, klanes]
                 col = column(c, h)
@@ -310,20 +463,7 @@
         ret[g, mine, :] = osend[g, mine, :]
 
     def stage(s, carry):
-        @pl.when(s < GROUPS)
-        def _():
-            lax.fori_loop(s * GP, (s + 1) * GP, project, 0)
-            send_state(0, s)
-
-        @pl.when(s == 0)
-        def _():
-            for d in range(1, BACK + 1):
-
-                @pl.when(tm >= d)
-                def _():
-                    a_copy(d).wait_recv()
-
-        for r, step in enumerate((round0, round1, round2)):
+        def turn(r, step):
             g = s - 1 - r
 
             @pl.when(jnp.logical_and(g >= 0, g < GROUPS))
@@ -335,6 +475,23 @@
                 else:
                     emit(g)
 
+        turn(2, round2)
+
+        @pl.when(s < GROUPS)
+        def _():
+            lax.fori_loop(s * GP, (s + 1) * GP, project, 0)
+            send_state(0, s)
+
+        @pl.when(s == 0)
+        def _():
+            for d in range(1, BACK + 1):
+
+                @pl.when(tm >= d)
+                def _():
+                    a_copy(d).wait_recv()
+
+        turn(1, round1)
+        turn(0, round0)
         return carry
 
     lax.fori_loop(0, GROUPS + 3, stage, 0)
@@ -356,21 +513,23 @@
 
     lax.fori_loop(0, GROUPS, finish, 0)
 
-    x_copy(0, every, every).wait_send()
-
-    def sent(g, carry):
-        q_copy(g, 0, every, every).wait_send()
+    whole(slotp, sps.at[0], spr.at[0]).wait_send()
+    whole(xp, xps.at[0], xpr.at[0]).wait_send()
+    whole(qp, qps.at[0], qpr.at[0]).wait_send()
+    whole(recvd.at[0:PEERS], ds_.at[0], dr.at[0]).wait_send()
+    for g in range(QUARTERS):
+        whole(recvx.at[half_every, :QW], xs.at[g], xr.at[g]).wait_send()
+    for j in range(PAIRS):
+        whole(recvq.at[j, half_every], qs.at[j], qr.at[j]).wait_send()
+    for g in range(GROUPS):
         o_copy(g, 0, every, every).wait_send()
-        for r in range(3):
-
-            @pl.when(tm + (1 << r) < TM)
-            def _():
-                s_copy(r, g).wait_send()
-
         out_copy(g).wait()
-        return carry
-
-    lax.fori_loop(0, GROUPS, sent, 0)
+    for r in range(3):
+
+        @pl.when(tm + (1 << r) < TM)
+        def _():
+            whole(ssend.at[r], ss.at[r], sr.at[r, 0]).wait_send()
+
     for d in range(1, BACK + 1):
 
         @pl.when(tm + d < TM)
@@ -391,13 +550,20 @@
             pltpu.VMEM((TOK, D), BF16),
             pltpu.VMEM((TOK, D), BF16),
             pltpu.VMEM((D, 2 * D), BF16),
-            pltpu.VMEM((ROWS, TOK), BF16),
+            pltpu.VMEM((ROWS + 128, TOK), BF16),
+            pltpu.VMEM((QUARTERS, 2, HALF * CAP, TOK), BF16),
             pltpu.VMEM((TOK, ROWS), BF16),
             pltpu.VMEM((TOK, ROWS), BF16),
-            pltpu.VMEM((ROWS, XW), BF16),
-            pltpu.VMEM((ROWS, XW), BF16),
-            pltpu.VMEM((GROUPS, ROWS, GW), BF16),
-            pltpu.VMEM((GROUPS, ROWS, GW), BF16),
+            pltpu.VMEM((8, TOK), F32),
+            pltpu.VMEM((QUARTERS, 8, TOK), F32),
+            pltpu.VMEM((QUARTERS, TOK, QW), BF16),
+            pltpu.VMEM((QUARTERS, 2, TOK, 256), BF16),
+            pltpu.VMEM((MEMBERS, H, 128), BF16),
+            pltpu.VMEM((MEMBERS, H, 128), BF16),
+            pltpu.VMEM((QUARTERS, 2, HALF * CAP, QW), BF16),
+            pltpu.VMEM((ROWS, D), BF16),
+            pltpu.VMEM((PAIRS, 2, HALF * CAP, 256), BF16),
+            pltpu.VMEM((PAIRS, ROWS, 256), BF16),
             pltpu.VMEM((PAIRS, ROWS, 256), BF16),
             pltpu.VMEM((PAIRS, ROWS, 256), BF16),
             pltpu.VMEM((GROUPS, ROWS, GW), BF16),
@@ -415,14 +581,22 @@
             pltpu.VMEM((3, H, HD, HD), BF16),
             dma((3,)),
             dma((1,)),
+            dma((QUARTERS,)),
             dma((1,)),
-            dma((GROUPS,)),
-            dma((GROUPS,)),
+            dma((QUARTERS,)),
+            dma((1,)),
+            dma((QUARTERS,)),
+            dma((1,)),
+            dma((1,)),
+            dma((QUARTERS,)),
+            dma((QUARTERS,)),
+            dma((PAIRS,)),
+            dma((PAIRS,)),
             dma((GROUPS,)),
             dma((GROUPS,)),
             dma((BACK,)),
             dma((BACK,)),
-            dma((3, GROUPS)),
+            dma((3,)),
             dma((3, GROUPS)),
             dma((GROUPS,)),
         ],

time: 121 us -> 115 us (0.950); the launches traced: 119 us -> 115 us
  Pallas kernels: 116 us -> 113 us
    pallas_call x1, Pallas kernels: 116 us -> 113 us  [on_device(): pl.pallas_call(kernel, out_shape=jax.ShapeDtypeStruct((TOK, D), BF16), in...]
where the time goes in v4:
time: 115 us
  Pallas kernels  113 us (98%)
  local copies, waits for them, and re-layouts  2.3 us (2%)
    pallas_call x1, Pallas kernels, on_device(): pl.pallas_call(kernel, out_shape=jax.ShapeDtypeStruct((TOK, D), BF16), in...  113 us
    unnamed x1, local copies, waits for them, and re-layouts  2.3 us

profile of v4, /device:TPU:4, one launch (start us, length us, event | category | flops | bytes accessed | tf_op | source)
XLA Modules:
  0.0 115.1 jit_solution(1290251870840204571)
XLA Ops:
  0.0 112.8 %memories.1 = bf16[256,2048]{1,0:T(8,128)(2,1)} custom-call(bf16[256,2048]{1,0:T(8,128)(2,1)} %tok_hbm.1, bf16[256,2048]{1,0:T(8,128)(2,1)} %qry_hbm.1, bf16[16,256]{1,0:T(8,128)(2,1)} %bitcast.3, s32[2,256]{1,0:T(2,128)} %bitcast.4, f32[2,256]{1,0:T(2,128)} %bitcast.5, bf16[1,2048,4096]{2,1,0:T(8,128)(2,1)} %w_hbm.1), custom_call_target="tpu_custom_call" | custom-call | tf_op jit(solution)/shard_map/memories/pallas_call | solution.py:544
  112.8 2.3 %copy.8 = bf16[256,2048]{1,0:T(8,128)(2,1)} copy(bf16[256,2048]{1,0:T(8,128)(2,1)} %memories.1) | data formatting | bytes 2097152

commit v5 on v4

--- a/solution.py
+++ b/solution.py
@@ -86,6 +86,16 @@
         ring = lax.rem(my + step, MEM_Y)
         return ring * MEM_Z + (other[g] if across else mz), across * 4 + ring
 
+    def in_turn(g, across, step):
+        swap = (g + 2) % QUARTERS
+        (place, number), (place2, number2) = in_half(g, across, step), in_half(swap, across, step)
+        return (
+            g + core * (swap - g),
+            place + core * (place2 - place),
+            number + core * (number2 - number),
+            partner[g] + core * (partner[swap] - partner[g]),
+        )
+
     def block(place):
         return pl.ds(pl.multiple_of(place * CAP, 16), CAP)
 
@@ -178,7 +188,7 @@
     def x_copy(g, own, src, dst, place):
         return pltpu.make_async_remote_copy(
             src_ref=sendx.at[g, own, src],
-            dst_ref=recvx.at[dst, g * QW : (g + 1) * QW],
+            dst_ref=recvx.at[dst, pl.ds(pl.multiple_of(g * QW, QW), QW)],
             send_sem=xs.at[g],
             recv_sem=xr.at[g],
             device_id=(tm, place),
@@ -271,10 +281,10 @@
     mine = block(me)
     for across, step in HALF_SHIFTS:
         for g in range(QUARTERS):
-            place, number = in_half(g, across, step)
+            quarter, place, number, mate = in_turn(g, across, step)
             for own in range(2):
-                dst = block(partner[g]) if own else mine
-                x_copy(g, own, block(number), dst, place).start()
+                dst = block(mate) if own else mine
+                x_copy(quarter, own, block(number), dst, place).start()
     load_w.start()
     for g in range(QUARTERS):
         number = in_half(g, 0, 0)[1]
@@ -294,10 +304,10 @@
             sendq[j, 1] = mm(picks[g, 1], qp[g, u]).astype(BF16)
         for across, step in HALF_SHIFTS:
             for g in range(QUARTERS):
-                place, number = in_half(g, across, step)
-                j = u * QUARTERS + g
+                quarter, place, number, mate = in_turn(g, across, step)
+                j = u * QUARTERS + quarter
                 for own in range(2):
-                    dst = block(partner[g]) if own else mine
+                    dst = block(mate) if own else mine
                     q_copy(j, own, block(number), dst, place).start()
         for g in range(QUARTERS):
             j = u * QUARTERS + g

time: 115 us -> 114 us (level)
  no operation moved by 1% of the time
where the time goes in v5:
time: 114 us
  Pallas kernels  112 us (98%)
  local copies, waits for them, and re-layouts  2.3 us (2%)
    pallas_call x1, Pallas kernels, on_device(): pl.pallas_call(kernel, out_shape=jax.ShapeDtypeStruct((TOK, D), BF16), in...  112 us
    unnamed x1, local copies, waits for them, and re-layouts  2.3 us

profile of v5, /device:TPU:4, one launch (start us, length us, event | category | flops | bytes accessed | tf_op | source)
XLA Modules:
  0.0 114.1 jit_solution(11825860081819063591)
XLA Ops:
  0.0 111.8 %memories.1 = bf16[256,2048]{1,0:T(8,128)(2,1)} custom-call(bf16[256,2048]{1,0:T(8,128)(2,1)} %tok_hbm.1, bf16[256,2048]{1,0:T(8,128)(2,1)} %qry_hbm.1, bf16[16,256]{1,0:T(8,128)(2,1)} %bitcast.3, s32[2,256]{1,0:T(2,128)} %bitcast.4, f32[2,256]{1,0:T(2,128)} %bitcast.5, bf16[1,2048,4096]{2,1,0:T(8,128)(2,1)} %w_hbm.1), custom_call_target="tpu_custom_call" | custom-call | tf_op jit(solution)/shard_map/memories/pallas_call | solution.py:554
  111.8 2.3 %copy.8 = bf16[256,2048]{1,0:T(8,128)(2,1)} copy(bf16[256,2048]{1,0:T(8,128)(2,1)} %memories.1) | data formatting | bytes 2097152

commit v6 on v5

--- a/solution.py
+++ b/solution.py
@@ -189,8 +189,8 @@
         return pltpu.make_async_remote_copy(
             src_ref=sendx.at[g, own, src],
             dst_ref=recvx.at[dst, pl.ds(pl.multiple_of(g * QW, QW), QW)],
-            send_sem=xs.at[g],
-            recv_sem=xr.at[g],
+            send_sem=xs.at[0],
+            recv_sem=xr.at[0],
             device_id=(tm, place),
             device_id_type=MESH,
         )
@@ -199,7 +199,7 @@
         return pltpu.make_async_remote_copy(
             src_ref=sendq.at[j, own, src],
             dst_ref=recvq.at[j, dst],
-            send_sem=qs.at[j],
+            send_sem=qs.at[0],
             recv_sem=qr.at[j],
             device_id=(tm, place),
             device_id_type=MESH,
@@ -209,7 +209,7 @@
         return pltpu.make_async_remote_copy(
             src_ref=osend.at[g, src],
             dst_ref=ret.at[g, dst],
-            send_sem=os_.at[g],
+            send_sem=os_.at[0],
             recv_sem=or_.at[g],
             device_id=(tm, to[i]),
             device_id_type=MESH,
@@ -371,8 +371,7 @@
             a_copy(d).start()
 
     load_w.wait()
-    for g in range(QUARTERS):
-        x_copy(g, 0, slice(0, CAP), half_every, to[0]).wait_recv()
+    whole(recvx.at[half_every], xs.at[0], xr.at[0]).wait_recv()
 
     lane = lax.broadcasted_iota(jnp.int32, (CHUNK, HD), 1)
 
@@ -468,7 +467,7 @@
             return inner
 
         lax.fori_loop(0, GH, head, 0)
-        for i in range(PEERS):
+        for i in reversed(range(PEERS)):
             o_copy(g, i, block(to[i]), mine).start()
         ret[g, mine, :] = osend[g, mine, :]
 
@@ -527,12 +526,10 @@
     whole(xp, xps.at[0], xpr.at[0]).wait_send()
     whole(qp, qps.at[0], qpr.at[0]).wait_send()
     whole(recvd.at[0:PEERS], ds_.at[0], dr.at[0]).wait_send()
-    for g in range(QUARTERS):
-        whole(recvx.at[half_every, :QW], xs.at[g], xr.at[g]).wait_send()
-    for j in range(PAIRS):
-        whole(recvq.at[j, half_every], qs.at[j], qr.at[j]).wait_send()
+    whole(recvx.at[half_every], xs.at[0], xr.at[0]).wait_send()
+    whole(recvq.at[0:HALF_PEERS], qs.at[0], qr.at[0]).wait_send()
+    whole(recvx.at[every], os_.at[0], or_.at[0]).wait_send()
     for g in range(GROUPS):
-        o_copy(g, 0, every, every).wait_send()
         out_copy(g).wait()
     for r in range(3):
 
@@ -598,11 +595,11 @@
             dma((QUARTERS,)),
             dma((1,)),
             dma((1,)),
-            dma((QUARTERS,)),
-            dma((QUARTERS,)),
+            dma((1,)),
+            dma((1,)),
+            dma((1,)),
             dma((PAIRS,)),
-            dma((PAIRS,)),
-            dma((GROUPS,)),
+            dma((1,)),
             dma((GROUPS,)),
             dma((BACK,)),
             dma((BACK,)),

time: 114 us -> 116 us (1.018); the launches traced: 114 us -> 115 us
  no operation moved by 1% of the time
where the time goes in v6:
time: 116 us; the launch traced here: 115 us
  Pallas kernels  112 us (97%)
  local copies, waits for them, and re-layouts  2.3 us (2%)
    pallas_call x1, Pallas kernels, on_device(): pl.pallas_call(kernel, out_shape=jax.ShapeDtypeStruct((TOK, D), BF16), in...  112 us

profile of v6, /device:TPU:4, one launch (start us, length us, event | category | flops | bytes accessed | tf_op | source)
XLA Modules:
  0.0 114.7 jit_solution(13664195476524599165)
XLA Ops:
  0.0 112.4 %memories.1 = bf16[256,2048]{1,0:T(8,128)(2,1)} custom-call(bf16[256,2048]{1,0:T(8,128)(2,1)} %tok_hbm.1, bf16[256,2048]{1,0:T(8,128)(2,1)} %qry_hbm.1, bf16[16,256]{1,0:T(8,128)(2,1)} %bitcast.3, s32[2,256]{1,0:T(2,128)} %bitcast.4, f32[2,256]{1,0:T(2,128)} %bitcast.5, bf16[1,2048,4096]{2,1,0:T(8,128)(2,1)} %w_hbm.1), custom_call_target="tpu_custom_call" | custom-call | tf_op jit(solution)/shard_map/memories/pallas_call | solution.py:551
  112.4 2.3 %copy.8 = bf16[256,2048]{1,0:T(8,128)(2,1)} copy(bf16[256,2048]{1,0:T(8,128)(2,1)} %memories.1) | data formatting | bytes 2097152
